TPU v7x, 512 devices: a whole 4x4x16 slice. The times are simulated.
512 devices in a mesh: past: 8 (over y, core), second: 64 (over z, x).
Axes of the slice: x: 4, y: 4, z: 16, core: 2. Of those that a mesh axis runs over, the one named last changes fastest.
Arguments:
- green_row: float32 [1024, 64, 128], P('second'), may hold values from -4 to 4
- green_hist: float32 [32, 1024, 64, 128], P('past', 'second'), may hold values from -5.25 to 5.25, as said below
- hamiltonian: float32 [64, 128], replicated, may hold values from -0.75 to 0.75
- quad_table: float32 [8], replicated, may hold values from 0.2 to 2
- weight_index: int32 [32], P('past'), may hold values from 0 to 7
- block_start: int32 [1], replicated, may hold values from 0 to 992
Outputs:
- green_next: float32 [1024, 64, 128], P('second')
- change_norm: float32 [1], replicated
Inputs may be any that keep to these rules, and one draw needn't show every extreme that they name: `green_hist`: real numbers of order one; magnitudes differ between second times.
All inputs are finite; a program needn't handle non-finite values.
Results may differ from a plain program's by a relative error of at most 0.0003.
Values sent between devices are 32-bit elements; how exact they have to be, the bound alone decides.
A program may use at most 64 MiB of HBM per device.

v0:
```python
import math

import jax
import jax.numpy as jnp
from jax import lax
from jax.sharding import PartitionSpec as P

coupling = 0.5
step_size = 0.25


def rotate(tiles, orbits):
    return jnp.concatenate([-tiles[..., orbits:], tiles[..., :orbits]], axis=-1)


def self_energy(tiles, orbits):
    magnitude = tiles[..., :orbits] ** 2 + tiles[..., orbits:] ** 2
    return -coupling * jnp.concatenate([magnitude, magnitude], axis=-1) * tiles


def local(green_row, green_hist, hamiltonian, quad_table, weight_index, block_start):
    orbits = hamiltonian.shape[0]
    sec_rows = green_row.shape[0]
    past_rows = green_hist.shape[0]
    total_past = past_rows * lax.axis_size("past")
    window_start = block_start[0]
    offset = lax.axis_index("second") * sec_rows
    past_first = lax.axis_index("past") * past_rows
    weights = jnp.take(quad_table, weight_index, axis=0)
    norm_scale = 1.0 / math.sqrt(orbits * total_past)
    ham_real = hamiltonian[:, :orbits]
    ham_imag = hamiltonian[:, orbits:]
    herm_real = 0.5 * (ham_real + ham_real.T)
    herm_imag = 0.5 * (ham_imag - ham_imag.T)
    right_side = jnp.stack([green_hist, self_energy(green_hist, orbits)])

    def select(tiles_in, wanted):
        local_pos = wanted - offset
        inside = (local_pos >= 0) & (local_pos < sec_rows)
        picked = jnp.take(tiles_in, jnp.clip(local_pos, 0, sec_rows - 1), axis=0)
        return jnp.where(inside[:, None, None], picked, jnp.zeros_like(picked))

    def window_of(tiles_in):
        wanted = window_start + jnp.arange(total_past, dtype=jnp.int32)
        every_tile = lax.psum(select(tiles_in, wanted), "second")
        return lax.dynamic_slice_in_dim(every_tile, past_first, past_rows, 0)

    def memory(tiles_in):
        window = window_of(tiles_in)
        weight_col = weights[:, None, None]
        left_side = jnp.stack([weight_col * self_energy(window, orbits), weight_col * window])
        left_side = jnp.stack([left_side[..., :orbits], left_side[..., orbits:]])
        contracted = jnp.einsum(
            "cqpij,qpsjk->csik", left_side, right_side, precision=lax.Precision.HIGHEST
        )
        return norm_scale * (contracted[0] + rotate(contracted[1], orbits))

    def derive(tiles_in, integral):
        first = jnp.einsum("ij,sjk->sik", herm_real, tiles_in, precision=lax.Precision.HIGHEST)
        second = jnp.einsum(
            "ij,sjk->sik", herm_imag, rotate(tiles_in, orbits), precision=lax.Precision.HIGHEST
        )
        combined = first + second + integral
        return jnp.concatenate([combined[..., orbits:], -combined[..., :orbits]], axis=-1)

    def summed(tiles_in):
        return lax.psum(memory(tiles_in), "past")

    slope_one = derive(green_row, summed(green_row))
    predicted = green_row + step_size * slope_one
    slope_two = derive(predicted, summed(predicted))
    green_next = green_row + 0.5 * step_size * (slope_one + slope_two)
    square_sum = lax.psum(jnp.sum((green_next - predicted) ** 2), "second")
    entry_count = sec_rows * lax.axis_size("second") * orbits * 2 * orbits
    change = jnp.sqrt(square_sum / entry_count) / step_size
    return (green_next, change.reshape(1))


def solution(mesh):
    placed = (P("second", None, None), P("past", "second", None, None), P(), P(), P("past"), P())
    return jax.shard_map(
        local, mesh=mesh, in_specs=placed, out_specs=(P("second", None, None), P()), check_vma=False
    )
```

profile of v0, /device:TPU:8, one launch (start us, length us, event | category | flops | bytes accessed | tf_op | source)
XLA Modules:
  0.0 879.2 jit_solution(6266481443964720765)
XLA Ops:
  7.2 0.0 copy-start
  7.2 0.0 all-reduce.5.cloned.1.call-start
  7.9 1.7 gather_fusion.1
  9.6 0.0 copy-start.11
  9.6 0.0 copy-start.1
  9.6 1.2 select_select_fusion.1
  10.8 0.0 all-reduce.5.cloned.1.call-update
  10.8 0.0 all-reduce.7.cloned.1.call-start
  10.9 0.0 copy-done.11
  10.9 0.0 copy-done
  10.9 0.6 gather_fusion
  11.6 0.0 copy-done.1
  11.6 1.0 slice_negate_fusion.5
  12.5 0.0 copy-done.2
  12.5 0.6 fusion.2
  13.1 2.7 copy_bitcast_fusion
  15.8 273.4 %all-reduce.5.cloned.1.call-done = f32[32,64,128]{2,1,0:T(8,128)} async-done(((f32[32,64,128]{2,1,0:T(8,128)}), f32[32,64,128]{2,1,0:T(8,128)}) %all-reduce.5.cloned.1.call-update) | async-done | bytes 1048592 | tf_op jit(solution)/shard_map/psum | solution.py:45
  289.2 1.1 fusion.28
  290.3 1.0 fusion.31
  291.3 0.1 maximum_bitcast_fusion.10
  291.5 4.4 fusion.5
  296.0 0.0 copy-start.10
  296.0 0.0 copy-start.8
  296.0 0.2 slice_negate_fusion.4
  296.2 1.0 fusion.14
  297.2 0.0 all-reduce.7.cloned.1.call-update
  297.2 0.0 all-reduce.9.cloned.1.call-start
  297.3 0.0 copy-done.10
  297.3 0.1 fusion.61
  297.4 0.1 copy.21
  297.4 0.1 copy.40
  297.5 0.0 copy-done.8
  297.5 0.7 convolution_bitcast_fusion
  298.3 67.6 %all-reduce.7.cloned.1.call-done = f32[16,64,128]{2,1,0:T(8,128)} async-done(((f32[16,64,128]{2,1,0:T(8,128)}), f32[16,64,128]{2,1,0:T(8,128)}) %all-reduce.7.cloned.1.call-update) | async-done | bytes 524304 | tf_op jit(solution)/shard_map/psum | solution.py:67
  365.9 1.6 fusion.8
  367.6 0.2 fusion.60
  367.8 0.0 copy-start.4
  367.8 0.0 copy-start.6
  367.8 0.8 copy-done.4
  368.6 0.2 copy-done.6
  368.8 0.2 multiply_add_fusion
  369.0 0.6 gather_fusion.2
  369.6 1.2 select_select_fusion
  370.8 0.0 all-reduce.9.cloned.1.call-update
  370.8 0.0 all-reduce.11.cloned.1.call-start
  370.9 1.4 fusion.38
  372.3 273.5 %all-reduce.9.cloned.1.call-done = f32[32,64,128]{2,1,0:T(8,128)} async-done(((f32[32,64,128]{2,1,0:T(8,128)}), f32[32,64,128]{2,1,0:T(8,128)}) %all-reduce.9.cloned.1.call-update) | async-done | bytes 1048592 | tf_op jit(solution)/shard_map/psum | solution.py:45
  645.8 1.1 fusion.27
  646.8 1.0 fusion.34
  647.9 0.1 maximum_bitcast_fusion.9
  648.0 0.0 copy-done.3
  648.0 4.1 fusion.6
  652.2 0.2 slice_negate_fusion.1
  652.4 1.0 fusion.12
  653.4 0.0 all-reduce.11.cloned.1.call-update
  653.5 0.2 slice_negate_fusion.2
  653.7 68.5 %all-reduce.11.cloned.1.call-done = f32[16,64,128]{2,1,0:T(8,128)} async-done(((f32[16,64,128]{2,1,0:T(8,128)}), f32[16,64,128]{2,1,0:T(8,128)}) %all-reduce.11.cloned.1.call-update) | async-done | bytes 524304 | tf_op jit(solution)/shard_map/psum | solution.py:67
  722.2 0.0 copy-done.9
  722.2 1.9 fusion.10
  724.1 0.2 fusion.59
  724.3 0.0 copy-done.5
  724.3 0.0 copy-done.7
  724.3 1.8 multiply_reduce_fusion
  726.1 144.7 %psum.39 = f32[]{:T(128)} all-reduce(f32[]{:T(128)} %get-tuple-element.3), channel_id=1, replica_groups=mesh['past'=8,'second'=64] {'second'}, use_global_device_ids=true, to_apply=%region_5.7 | all-reduce | flops 1 | bytes 8 | tf_op jit(solution)/shard_map/psum | solution.py:73
  (12 shorter events, 0.1 us)
Async XLA Ops:
  7.2 3.7 copy-start
  7.2 282.0 %all-reduce.5.cloned.1.call-start = ((), (), s32[]{:S(2)}) async-start(), calls=%async_computation | async-start | bytes 2097152 | tf_op jit(solution)/shard_map/psum | solution.py:45
  9.6 1.3 copy-start.11
  9.6 2.0 copy-start.1
  10.8 1.7 copy-start.2
  10.8 355.1 %all-reduce.7.cloned.1.call-start = ((), (), s32[]{:S(2)}) async-start(), calls=%async_computation.1 | async-start | bytes 1048576 | tf_op jit(solution)/shard_map/psum | solution.py:67
  296.0 1.3 copy-start.10
  296.0 1.6 copy-start.8
  297.2 348.5 %all-reduce.9.cloned.1.call-start = ((), (), s32[]{:S(2)}) async-start(), calls=%async_computation.2 | async-start | bytes 2097152 | tf_op jit(solution)/shard_map/psum | solution.py:45
  367.8 0.8 copy-start.4
  367.8 1.0 copy-start.6
  370.8 277.2 %copy-start.3 = (f32[1,4,16,64,128]{4,3,0,1,2:T(8,128)S(1)}, f32[1,4,16,64,128]{4,3,0,1,2:T(8,128)}, u32[]{:S(2)}) copy-start(f32[1,4,16,64,128]{4,3,0,1,2:T(8,128)} %get-tuple-element.7) | copy-start | bytes 6291460
  370.8 351.4 %all-reduce.11.cloned.1.call-start = ((), (), s32[]{:S(2)}) async-start(), calls=%async_computation.3 | async-start | bytes 1048576 | tf_op jit(solution)/shard_map/psum | solution.py:67
  652.4 69.8 %copy-start.9 = (f32[16,128,64]{1,2,0:T(8,128)S(1)}, f32[16,128,64]{1,2,0:T(8,128)}, u32[]{:S(2)}) copy-start(f32[16,128,64]{1,2,0:T(8,128)} %fusion.38) | copy-start | bytes 1572868
  722.2 2.1 copy-start.5
  722.2 2.1 copy-start.7
Sparse Core Ops, SparseCore 0:
  11.4 277.7 all-reduce.4
  297.4 68.5 all-reduce.6
  370.9 274.7 all-reduce.8
  653.6 68.5 all-reduce.10
where the time goes:
time: 880 us; the launch traced here: 879 us
  waiting for transfers between devices  683 us (78%)
  blocking collectives  145 us (16%)
  between operations  16.5 us (2%)
  other arithmetic  16.1 us (2%)
  matrix products  14.3 us (2%)
    psum x2, waiting for transfers between devices, window_of(): every_tile = lax.psum(select(tiles_in, wanted), 'second')  547 us
    psum x1, blocking collectives, local(): square_sum = lax.psum(jnp.sum((green_next - predicted) ** 2), 'second')  145 us
    psum x2, waiting for transfers between devices, summed(): return lax.psum(memory(tiles_in), 'past')  136 us
  transfers between devices with their start and end apart: 4, of which 4 were waited for; matrix products, arithmetic and copies ran while one was open for 1% of the time, Pallas kernels for 0%

commit v1 on v0

v1 whole, which is shorter than its diff:
```python
import functools
import math

import jax
import jax.numpy as jnp
from jax import lax
from jax.experimental import pallas as pl
from jax.experimental.pallas import tpu as pltpu
from jax.sharding import PartitionSpec as P

COUPLING = 0.5
STEP = 0.25
CHIPS_X = 4
LANES = 128
MESH = pl.DeviceIdType.MESH
F32 = jnp.float32
BF16 = jnp.bfloat16


def wait_bytes(ref, sem):
    pltpu.make_async_copy(ref, ref, sem).wait()


def send(src, dst, send_sem, recv_sem, where):
    pltpu.make_async_remote_copy(
        src_ref=src, dst_ref=dst, send_sem=send_sem, recv_sem=recv_sem, device_id=where, device_id_type=MESH
    ).start()


def split(values):
    high = values.astype(BF16).astype(F32)
    return high, values - high


def kernel(
    dims, start_ref, index_ref, table_ref, row_hbm, hist_hbm, ham_ref, out_ref, norm_ref,
    row, hist, r_high, r_low, r_ham, left, l_ham, cx, rx, sx, zs, rz, win,
    part, rc, sc, ry, slope, pred, norm_p, norm_x, norm_z,
    in_sem, x_sem, a_sem, z_sem, gz_sem, gx_sem, c_send, c_recv, y_send, y_recv,
    oy_send, oy_recv, oc_send, oc_recv, n_sem,
):
    n_past, n_x, n_z, chunks, slots, tiles, groups, norm_scale, entries = dims
    n_y = n_past // 2
    size = tiles // groups
    half = LANES // 2
    q, sec = lax.axis_index("past"), lax.axis_index("second")
    z, x = sec // n_x, sec % n_x
    y, core = q // 2, q % 2
    mine = z % chunks
    rows = row.shape[2]

    def at_x(x_to):
        return (q, z * n_x + x_to)

    def at_z(z_to):
        return (q, z_to * n_x + x)

    def at_past(past_to):
        return (past_to, sec)

    partner = at_past(2 * y + (1 - core))

    row_copy = pltpu.make_async_copy(row_hbm, row, in_sem.at[0])
    row_copy.start()
    hist_copy = pltpu.make_async_copy(hist_hbm, hist, in_sem.at[1])
    hist_copy.start()

    barrier = pltpu.get_barrier_semaphore()
    others = [at_x((x + d) % n_x) for d in range(1, n_x)]
    others += [at_past((q + d) % n_past) for d in range(1, n_past)]
    others += [at_z((z + d) % n_z) for d in range(1, n_z)]
    for other in others:
        pl.semaphore_signal(barrier, inc=1, device_id=other, device_id_type=MESH)

    lane = lax.broadcasted_iota(jnp.int32, (1, LANES), 1)
    real = lane < half
    turn = jnp.where(real, F32(1), F32(-1))

    def swap(values):
        return pltpu.roll(values, half, axis=values.ndim - 1)

    def self_energy(values):
        square = values * values
        return (square + swap(square)) * values * F32(-COUPLING)


    def scatter_x(k):
        for d in range(1, n_x):
            to = (x + d) % n_x
            send(cx.at[k, to], rx.at[k, d - 1], x_sem.at[k, 0], x_sem.at[k, 1], at_x(to))

    def sum_x(k):
        wait_bytes(rx.at[k], x_sem.at[k, 1])
        total = cx[k, x]
        for d in range(n_x - 1):
            total = total + rx[k, d]
        return total

    def scatter_z(k):
        for d in range(1, n_z):
            to = (z + d) % n_z
            send(zs.at[k, to % chunks], rz.at[k, d - 1], z_sem.at[k, 0], z_sem.at[k, 1], at_z(to))

    def gather_z(k):
        wait_bytes(rz.at[k], z_sem.at[k, 1])
        total = zs[k, mine]
        for d in range(n_z - 1):
            total = total + rz[k, d]
        win[k, x, mine] = total
        for e in range(1 - chunks // 2, chunks // 2 + 1):
            if e != 0:
                block = win.at[k, x, mine]
                send(block, block, gz_sem.at[k, 0], gz_sem.at[k, 1], at_z((z + e + n_z) % n_z))

    def gather_x(k):
        wait_bytes(win.at[k, 0, pl.ds(0, chunks - 1)], gz_sem.at[k, 1])
        for d in range(1, n_x):
            block = win.at[k, x]
            send(block, block, gx_sem.at[k, 0], gx_sem.at[k, 1], at_x((x + d) % n_x))

    def window_done(k):
        wait_bytes(win.at[k, pl.ds(0, n_x - 1)], gx_sem.at[k, 1])


    def prepare_hist(first, last):
        def body(s, carry):
            columns = pl.ds(pl.multiple_of(s * LANES, LANES), LANES)
            for p in range(slots):
                tile = hist[p, s]
                for kind, values in enumerate((tile, self_energy(tile))):
                    high, low = split(values)
                    at = pl.ds((2 * p + kind) * half, half)
                    r_high[at, columns] = high.astype(BF16)
                    r_low[at, columns] = low.astype(BF16)
            return carry

        lax.fori_loop(first, last, body, 0)

    def prepare_ham():
        tile = ham_ref[...]
        flipped = jnp.concatenate([tile, jnp.zeros_like(tile)], axis=0).T
        ham = F32(0.5) * (tile * turn + flipped[:half] + swap(flipped[half:]))
        slope[pl.ds(0, n_past)] = ham.reshape(n_past, rows, LANES)

    def prepare_left_ham():
        high, low = split(slope[q])
        blank = jnp.zeros((LANES - 3 * rows, LANES), F32)
        l_ham[...] = jnp.concatenate([high, high, low, blank], axis=0).T.astype(BF16)
        r_ham[...] = jnp.zeros(r_ham.shape, BF16)

    def prepare_right_ham(s, values):
        high, low = split(values)
        both = jnp.concatenate([high, low, high, jnp.zeros_like(high)], axis=0)
        r_ham[pl.ds(0, 4 * rows), pl.ds(s * LANES, LANES)] = both.astype(BF16)

    def prepare_left(k):
        for t in range(slots):
            weight = table_ref[index_ref[t]] * F32(norm_scale)
            tile = win[k, t].reshape(half, LANES)
            first = weight * self_energy(tile)
            second = weight * tile
            real_part = jnp.where(real, first, swap(second))
            imag_part = jnp.where(real, swap(first), second)
            high, low = split(jnp.concatenate([real_part, imag_part], axis=0))
            left[pl.ds(0, LANES), pl.ds(t * LANES, LANES)] = high.astype(BF16)
            left[pl.ds(LANES, LANES), pl.ds(t * LANES, LANES)] = low.astype(BF16)

    def contract(k, g):
        columns = pl.ds(g * size * LANES, size * LANES)
        both = jnp.dot(left[...], r_high[:, columns], preferred_element_type=F32)
        more = jnp.dot(left[pl.ds(0, LANES), :], r_low[:, columns], preferred_element_type=F32)
        ham = jnp.dot(l_ham[...], r_ham[:, columns], preferred_element_type=F32)
        total = both[:LANES] + both[LANES:] + more + ham
        for s in range(size):
            at = slice(s * LANES, (s + 1) * LANES)
            tile = total[:half, at] - turn * swap(total[half:, at])
            for p in range(n_past):
                part[k, g, p % 2, p // 2, s] = tile[p * rows : (p + 1) * rows]
        send(part.at[k, g, 1 - core], rc.at[k, g], c_send.at[k, g], c_recv.at[k, g], partner)

    def between_chips(k, g):
        wait_bytes(rc.at[k, g], c_recv.at[k, g])
        sc[k, g] = part[k, g, core] + rc[k, g]
        for d in range(1, n_y):
            to = (y + d) % n_y
            send(sc.at[k, g, to], ry.at[k, g, d - 1], y_send.at[k, g], y_recv.at[k, g], at_past(2 * to + core))

    def slope_of(k, g):
        wait_bytes(ry.at[k, g], y_recv.at[k, g])
        total = sc[k, g, y]
        for d in range(n_y - 1):
            total = total + ry[k, g, d]
        return turn * swap(total.reshape(size * rows, LANES)).reshape(size, rows, LANES)

    def run(k, finish):
        for g in range(groups + 2):
            if g < groups:
                contract(k, g)
            if 0 <= g - 1 < groups:
                between_chips(k, g - 1)
            if 0 <= g - 2 < groups:
                finish(g - 2, slope_of(k, g - 2))


    start = start_ref[0]
    row_copy.wait()
    for t in range(slots):
        wanted = start + slots * q + t - tiles * sec
        inside = (wanted >= 0) & (wanted < tiles)
        tile = row[jnp.clip(wanted, 0, tiles - 1)]
        cx[0, t] = jnp.where(inside, tile, jnp.zeros_like(tile))
    pl.semaphore_wait(barrier, len(others))
    scatter_x(0)
    prepare_ham()
    prepare_left_ham()
    for s in range(tiles):
        prepare_right_ham(s, row[s, q])
    zs[0] = sum_x(0).reshape(zs.shape[1:])
    scatter_z(0)
    hist_copy.wait()
    prepare_hist(0, tiles // 2)
    gather_z(0)
    prepare_hist(tiles // 2, tiles)
    gather_x(0)
    window_done(0)
    prepare_left(0)

    def finish_first(g, values):
        for i in range(size):
            s = g * size + i
            slope[s] = values[i]
            ahead = row[s, q] + F32(STEP) * values[i]
            pred[s] = ahead

    run(0, finish_first)


    for p in range(slots * n_past):
        wanted = start + p - tiles * sec
        inside = (wanted >= 0) & (wanted < tiles)
        tile = pred[jnp.clip(wanted, 0, tiles - 1)]
        cx[1, p % slots, p // slots] = jnp.where(inside, tile, jnp.zeros_like(tile))
    scatter_x(1)
    for s in range(tiles):
        prepare_right_ham(s, pred[s])
    sx[...] = sum_x(1)
    for d in range(1, n_past):
        to = (q + d) % n_past
        send(sx.at[to], zs.at[1, q], a_sem.at[0], a_sem.at[1], at_past(to))
    zs[1, q] = sx[q]
    wait_bytes(zs.at[1, pl.ds(0, n_past - 1)], a_sem.at[1])
    scatter_z(1)
    gather_z(1)
    gather_x(1)
    window_done(1)
    prepare_left(1)

    def to_chips(g, values):
        squares = jnp.zeros((rows, LANES), F32)
        for i in range(size):
            s = g * size + i
            after = row[s, q] + F32(0.5 * STEP) * (slope[s] + values[i])
            out_ref[s, y, core] = after
            change = after - pred[s]
            squares = squares + change * change
        norm_p[q] = (norm_p[q] if g else 0) + jnp.sum(squares, axis=0, keepdims=True)
        block = out_ref.at[pl.ds(g * size, size), y, core]
        for d in range(1, n_y):
            send(block, block, oy_send.at[g], oy_recv.at[g], at_past(2 * ((y + d) % n_y) + core))

    run(1, to_chips)

    def share(buffer, own, number, n, where):
        for d in range(1, n):
            block = buffer.at[own]
            send(block, block, n_sem.at[number, 0], n_sem.at[number, 1], where((own + d) % n))

    def shared(buffer, number, n):
        wait_bytes(buffer.at[pl.ds(0, n - 1)], n_sem.at[number, 1])
        total = buffer[0]
        for i in range(1, n):
            total = total + buffer[i]
        return total

    share(norm_p, q, 0, n_past, at_past)
    for g in range(groups):
        wait_bytes(rc.at[0, g, pl.ds(0, n_y - 1)], oy_recv.at[g])
        block = out_ref.at[pl.ds(g * size, size), :, core]
        send(block, block, oc_send.at[g], oc_recv.at[g], partner)
    norm_x[x] = shared(norm_p, 0, n_past)
    share(norm_x, x, 1, n_x, at_x)
    norm_z[z] = shared(norm_x, 1, n_x)
    share(norm_z, z, 2, n_z, at_z)
    total = shared(norm_z, 2, n_z)
    mean = jnp.sum(total, axis=1, keepdims=True) * F32(1.0 / entries)
    norm_ref[0] = (jnp.sqrt(jnp.broadcast_to(mean, (1, LANES))) * F32(1.0 / STEP))[0, 0]
    for g in range(groups):
        wait_bytes(rc.at[0, g], oc_recv.at[g])

    for k in range(2):
        wait_bytes(rx.at[k], x_sem.at[k, 0])
        wait_bytes(rz.at[k], z_sem.at[k, 0])
        wait_bytes(win.at[k, 0, pl.ds(0, chunks - 1)], gz_sem.at[k, 0])
        wait_bytes(win.at[k, pl.ds(0, n_x - 1)], gx_sem.at[k, 0])
        for g in range(groups):
            wait_bytes(rc.at[k, g], c_send.at[k, g])
            wait_bytes(ry.at[k, g], y_send.at[k, g])
    for g in range(groups):
        wait_bytes(rc.at[0, g, pl.ds(0, n_y - 1)], oy_send.at[g])
        wait_bytes(rc.at[0, g], oc_send.at[g])
    wait_bytes(zs.at[1, pl.ds(0, n_past - 1)], a_sem.at[0])
    wait_bytes(norm_p.at[pl.ds(0, n_past - 1)], n_sem.at[0, 0])
    wait_bytes(norm_x.at[pl.ds(0, n_x - 1)], n_sem.at[1, 0])
    wait_bytes(norm_z.at[pl.ds(0, n_z - 1)], n_sem.at[2, 0])


def local(n_past, n_second, green_row, green_hist, hamiltonian, quad_table, weight_index, block_start):
    tiles, orbits, _ = green_row.shape
    slots = green_hist.shape[0]
    n_x = CHIPS_X
    n_z = n_second // n_x
    n_y = n_past // 2
    rows = orbits // n_past
    chunks = n_past
    groups = 4 if tiles % 4 == 0 and tiles > 4 else 2
    size = tiles // groups
    depth = 2 * slots * orbits
    dims = (
        n_past, n_x, n_z, chunks, slots, tiles, groups,
        1.0 / math.sqrt(orbits * slots * n_past), tiles * n_second * orbits * 2 * orbits,
    )
    dma = pltpu.SemaphoreType.DMA
    scratch = [
        pltpu.VMEM((tiles, n_past, rows, LANES), F32),
        pltpu.VMEM((slots, tiles, orbits, LANES), F32),
        pltpu.VMEM((depth, tiles * LANES), BF16),
        pltpu.VMEM((depth, tiles * LANES), BF16),
        pltpu.VMEM((LANES, tiles * LANES), BF16),
        pltpu.VMEM((2 * LANES, depth), BF16),
        pltpu.VMEM((LANES, LANES), BF16),
        pltpu.VMEM((2, n_x, n_past, rows, LANES), F32),
        pltpu.VMEM((2, n_x - 1, n_past, rows, LANES), F32),
        pltpu.VMEM((n_past, rows, LANES), F32),
        pltpu.VMEM((2, chunks, rows, LANES), F32),
        pltpu.VMEM((2, n_z - 1, rows, LANES), F32),
        pltpu.VMEM((2, slots, chunks, rows, LANES), F32),
        pltpu.VMEM((2, groups, 2, n_y, size, rows, LANES), F32),
        pltpu.VMEM((2, groups, n_y, size, rows, LANES), F32),
        pltpu.VMEM((2, groups, n_y, size, rows, LANES), F32),
        pltpu.VMEM((2, groups, n_y - 1, size, rows, LANES), F32),
        pltpu.VMEM((max(tiles, n_past), rows, LANES), F32),
        pltpu.VMEM((tiles, rows, LANES), F32),
        pltpu.VMEM((n_past, 1, LANES), F32),
        pltpu.VMEM((n_x, 1, LANES), F32),
        pltpu.VMEM((n_z, 1, LANES), F32),
        dma((2,)),
        dma((2, 2)),
        dma((2,)),
        dma((2, 2)),
        dma((2, 2)),
        dma((2, 2)),
        dma((2, groups)), dma((2, groups)),
        dma((2, groups)), dma((2, groups)),
        dma((groups,)), dma((groups,)),
        dma((groups,)), dma((groups,)),
        dma((3, 2)),
    ]
    smem = pl.BlockSpec(memory_space=pltpu.SMEM)
    vmem = pl.BlockSpec(memory_space=pltpu.VMEM)
    anywhere = pl.BlockSpec(memory_space=pl.ANY)
    after, change = pl.pallas_call(
        functools.partial(kernel, dims),
        out_shape=(
            jax.ShapeDtypeStruct((tiles, n_y, 2, rows, LANES), F32),
            jax.ShapeDtypeStruct((1,), F32),
        ),
        in_specs=[smem, smem, smem, anywhere, anywhere, vmem],
        out_specs=(vmem, smem),
        scratch_shapes=scratch,
        compiler_params=pltpu.CompilerParams(
            collective_id=0, has_side_effects=True, vmem_limit_bytes=40 * 1024 * 1024
        ),
    )(
        block_start, weight_index, quad_table,
        green_row.reshape(tiles, n_past, rows, LANES), green_hist, hamiltonian,
    )
    return after.reshape(tiles, orbits, LANES), change


def solution(mesh):
    placed = (P("second", None, None), P("past", "second", None, None), P(), P(), P("past"), P())
    return jax.shard_map(
        functools.partial(local, mesh.shape["past"], mesh.shape["second"]),
        mesh=mesh,
        in_specs=placed,
        out_specs=(P("second", None, None), P()),
        check_vma=False,
    )
```

time: 880 us -> 109 us (0.12)
  the two profiles are of different devices: /device:TPU:8 before, /device:TPU:1 now
where the time goes in v1:
time: 109 us; the launch traced here: 108 us
  Pallas kernels  99.8 us (92%)
  local copies, waits for them, and re-layouts  5.49 us (5%)
  between operations  2.99 us (3%)
    pallas_call x1, Pallas kernels, local(): pl.pallas_call(functools.partial(kernel, dims), out_shape=(jax.ShapeDtype...  99.8 us
    unnamed x11, local copies, waits for them, and re-layouts  5.49 us

profile of v1, /device:TPU:1, one launch (start us, length us, event | category | flops | bytes accessed | tf_op | source)
XLA Modules:
  0.0 108.3 jit_solution(3570898152231310742)
XLA Ops:
  1.3 0.0 copy-start
  1.3 1.6 %copy-done = f32[4,16,64,128]{3,2,1,0:T(8,128)S(1)} copy-done((f32[4,16,64,128]{3,2,1,0:T(8,128)S(1)}, f32[4,16,64,128]{3,2,1,0:T(8,128)}, u32[]{:S(2)}) %copy-start) | copy-done | bytes 2097176
  2.9 0.0 copy-start.1
  2.9 1.0 copy-done.1
  3.9 0.0 copy-start.2
  3.9 0.8 copy-done.2
  4.7 0.0 copy-start.3
  4.7 0.7 copy-done.3
  5.3 0.0 copy-start.4
  5.3 0.7 copy-done.4
  6.0 99.8 %shard_map.77 = (f32[16,4,2,8,128]{4,3,2,1,0:T(8,128)S(1)}, f32[1]{0:T(128)}) custom-call(s32[1]{0:T(128)S(6)} %copy.10.start_ref, s32[4]{0:T(128)S(1)} %copy-done.3, f32[8]{0:T(128)S(1)} %copy-done.4, f32[16,8,8,128]{3,2,1,0:T(8,128)S(1)} %bitcast.3, f32[4,16,64,128]{3,2,1,0:T(8,128)S(1)} %copy-done, f32[64,128]{1,0:T(8,128)S(1)} %copy-done.2), custom_call_target="tpu_custom_call" | custom-call | tf_op jit(solution)/shard_map/pallas_call | solution.py:371
  105.8 0.8 copy.11
Async XLA Ops:
  1.3 1.6 %copy-start = (f32[4,16,64,128]{3,2,1,0:T(8,128)S(1)}, f32[4,16,64,128]{3,2,1,0:T(8,128)}, u32[]{:S(2)}) copy-start(f32[4,16,64,128]{3,2,1,0:T(8,128)} %hist_hbm.1) | copy-start | bytes 6291460
  2.9 1.0 copy-start.1
  3.9 0.8 copy-start.2
  4.7 0.7 copy-start.3
  5.3 0.7 copy-start.4

commit v2 on v1

--- a/solution.py
+++ b/solution.py
@@ -27,6 +27,10 @@
     ).start()
 
 
+def far_first(n):
+    return sorted(range(1, n), key=lambda d: -min(d, n - d))
+
+
 def split(values):
     high = values.astype(BF16).astype(F32)
     return high, values - high
@@ -34,9 +38,9 @@
 
 def kernel(
     dims, start_ref, index_ref, table_ref, row_hbm, hist_hbm, ham_ref, out_ref, norm_ref,
-    row, hist, r_high, r_low, r_ham, left, l_ham, cx, rx, sx, zs, rz, win,
-    part, rc, sc, ry, slope, pred, norm_p, norm_x, norm_z,
-    in_sem, x_sem, a_sem, z_sem, gz_sem, gx_sem, c_send, c_recv, y_send, y_recv,
+    row, hist, r_high, r_low, r_ham, left, l_ham, cx, rx, rp, zs, rz, win,
+    part, rc, sc, ry, slope, pred, norm_p, norm_z,
+    in_sem, x_sem, a_sem, z_sem, g_sem, c_send, c_recv, y_send, y_recv,
     oy_send, oy_recv, oc_send, oc_recv, n_sem,
 ):
     n_past, n_x, n_z, chunks, slots, tiles, groups, norm_scale, entries = dims
@@ -58,6 +62,11 @@
     def at_past(past_to):
         return (past_to, sec)
 
+    def at_plane(d):
+        return (2 * ((y + d[0]) % n_y) + (core + d[1]) % 2, z * n_x + (x + d[2]) % n_x)
+
+    plane = [(a, b, c) for a in range(n_y) for b in range(2) for c in range(n_x)][1:]
+    plane.sort(key=lambda d: -min(d[0], n_y - d[0]) - min(d[2], n_x - d[2]))
     partner = at_past(2 * y + (1 - core))
 
     row_copy = pltpu.make_async_copy(row_hbm, row, in_sem.at[0])
@@ -66,9 +75,15 @@
     hist_copy.start()
 
     barrier = pltpu.get_barrier_semaphore()
-    others = [at_x((x + d) % n_x) for d in range(1, n_x)]
-    others += [at_past((q + d) % n_past) for d in range(1, n_past)]
-    others += [at_z((z + d) % n_z) for d in range(1, n_z)]
+    reach = min(chunks // 2, n_z // 2)
+    others = [at_z((z + d) % n_z) for d in far_first(n_z)]
+    others += [
+        (q, (z + e) % n_z * n_x + (x + d) % n_x)
+        for e in far_first(n_z)
+        if min(e, n_z - e) <= reach
+        for d in range(1, n_x)
+    ]
+    others += [at_plane(d) for d in plane]
     for other in others:
         pl.semaphore_signal(barrier, inc=1, device_id=other, device_id_type=MESH)
 
@@ -84,42 +99,52 @@
         return (square + swap(square)) * values * F32(-COUPLING)
 
 
-    def scatter_x(k):
-        for d in range(1, n_x):
+    def scatter_x():
+        for d in far_first(n_x):
             to = (x + d) % n_x
-            send(cx.at[k, to], rx.at[k, d - 1], x_sem.at[k, 0], x_sem.at[k, 1], at_x(to))
-
-    def sum_x(k):
-        wait_bytes(rx.at[k], x_sem.at[k, 1])
-        total = cx[k, x]
+            send(cx.at[0, to], rx.at[d - 1], x_sem.at[0], x_sem.at[1], at_x(to))
+
+    def sum_x():
+        wait_bytes(rx, x_sem.at[1])
+        total = cx[0, x]
         for d in range(n_x - 1):
-            total = total + rx[k, d]
+            total = total + rx[d]
         return total
 
+    def scatter_plane():
+        for d in plane:
+            to, column = at_plane(d)
+            block = cx.at[1, column % n_x, to]
+            send(block, rp.at[x * n_past + q], a_sem.at[0], a_sem.at[1], (to, column))
+        rp[x * n_past + q] = cx[1, x, q]
+
+    def sum_plane():
+        wait_bytes(rp.at[pl.ds(0, n_x * n_past - 1)], a_sem.at[1])
+        total = rp[pl.ds(0, n_past)]
+        for i in range(1, n_x):
+            total = total + rp[pl.ds(i * n_past, n_past)]
+        return total
+
     def scatter_z(k):
-        for d in range(1, n_z):
+        for d in far_first(n_z):
             to = (z + d) % n_z
             send(zs.at[k, to % chunks], rz.at[k, d - 1], z_sem.at[k, 0], z_sem.at[k, 1], at_z(to))
 
-    def gather_z(k):
+    def gather(k):
         wait_bytes(rz.at[k], z_sem.at[k, 1])
         total = zs[k, mine]
         for d in range(n_z - 1):
             total = total + rz[k, d]
-        win[k, x, mine] = total
-        for e in range(1 - chunks // 2, chunks // 2 + 1):
-            if e != 0:
-                block = win.at[k, x, mine]
-                send(block, block, gz_sem.at[k, 0], gz_sem.at[k, 1], at_z((z + e + n_z) % n_z))
-
-    def gather_x(k):
-        wait_bytes(win.at[k, 0, pl.ds(0, chunks - 1)], gz_sem.at[k, 1])
-        for d in range(1, n_x):
-            block = win.at[k, x]
-            send(block, block, gx_sem.at[k, 0], gx_sem.at[k, 1], at_x((x + d) % n_x))
+        win[k, x * chunks + mine] = total
+        block = win.at[k, x * chunks + mine]
+        for e in sorted(range(1 - chunks // 2, chunks // 2 + 1), key=lambda e: -abs(e)):
+            for d in far_first(n_x) + [0]:
+                if d or e:
+                    where = (q, (z + e + n_z) % n_z * n_x + (x + d) % n_x)
+                    send(block, block, g_sem.at[k, 0], g_sem.at[k, 1], where)
 
     def window_done(k):
-        wait_bytes(win.at[k, pl.ds(0, n_x - 1)], gx_sem.at[k, 1])
+        wait_bytes(win.at[k, pl.ds(0, slots * chunks - 1)], g_sem.at[k, 1])
 
 
     def prepare_hist(first, last):
@@ -156,7 +181,7 @@
     def prepare_left(k):
         for t in range(slots):
             weight = table_ref[index_ref[t]] * F32(norm_scale)
-            tile = win[k, t].reshape(half, LANES)
+            tile = win[k, pl.ds(t * chunks, chunks)].reshape(half, LANES)
             first = weight * self_energy(tile)
             second = weight * tile
             real_part = jnp.where(real, first, swap(second))
@@ -181,7 +206,7 @@
     def between_chips(k, g):
         wait_bytes(rc.at[k, g], c_recv.at[k, g])
         sc[k, g] = part[k, g, core] + rc[k, g]
-        for d in range(1, n_y):
+        for d in far_first(n_y):
             to = (y + d) % n_y
             send(sc.at[k, g, to], ry.at[k, g, d - 1], y_send.at[k, g], y_recv.at[k, g], at_past(2 * to + core))
 
@@ -193,13 +218,13 @@
         return turn * swap(total.reshape(size * rows, LANES)).reshape(size, rows, LANES)
 
     def run(k, finish):
-        for g in range(groups + 2):
+        for g in range(groups + 1):
             if g < groups:
                 contract(k, g)
-            if 0 <= g - 1 < groups:
+            if g >= 1:
                 between_chips(k, g - 1)
-            if 0 <= g - 2 < groups:
-                finish(g - 2, slope_of(k, g - 2))
+        for g in range(groups):
+            finish(g, slope_of(k, g))
 
 
     start = start_ref[0]
@@ -210,18 +235,17 @@
         tile = row[jnp.clip(wanted, 0, tiles - 1)]
         cx[0, t] = jnp.where(inside, tile, jnp.zeros_like(tile))
     pl.semaphore_wait(barrier, len(others))
-    scatter_x(0)
+    scatter_x()
     prepare_ham()
     prepare_left_ham()
     for s in range(tiles):
         prepare_right_ham(s, row[s, q])
-    zs[0] = sum_x(0).reshape(zs.shape[1:])
+    zs[0] = sum_x().reshape(zs.shape[1:])
     scatter_z(0)
     hist_copy.wait()
     prepare_hist(0, tiles // 2)
-    gather_z(0)
+    gather(0)
     prepare_hist(tiles // 2, tiles)
-    gather_x(0)
     window_done(0)
     prepare_left(0)
 
@@ -240,18 +264,12 @@
         inside = (wanted >= 0) & (wanted < tiles)
         tile = pred[jnp.clip(wanted, 0, tiles - 1)]
         cx[1, p % slots, p // slots] = jnp.where(inside, tile, jnp.zeros_like(tile))
-    scatter_x(1)
+    scatter_plane()
     for s in range(tiles):
         prepare_right_ham(s, pred[s])
-    sx[...] = sum_x(1)
-    for d in range(1, n_past):
-        to = (q + d) % n_past
-        send(sx.at[to], zs.at[1, q], a_sem.at[0], a_sem.at[1], at_past(to))
-    zs[1, q] = sx[q]
-    wait_bytes(zs.at[1, pl.ds(0, n_past - 1)], a_sem.at[1])
+    zs[1] = sum_plane()
     scatter_z(1)
-    gather_z(1)
-    gather_x(1)
+    gather(1)
     window_done(1)
     prepare_left(1)
 
@@ -263,17 +281,12 @@
             out_ref[s, y, core] = after
             change = after - pred[s]
             squares = squares + change * change
-        norm_p[q] = (norm_p[q] if g else 0) + jnp.sum(squares, axis=0, keepdims=True)
+        norm_p[x * n_past + q] = (norm_p[x * n_past + q] if g else 0) + jnp.sum(squares, axis=0, keepdims=True)
         block = out_ref.at[pl.ds(g * size, size), y, core]
-        for d in range(1, n_y):
+        for d in far_first(n_y):
             send(block, block, oy_send.at[g], oy_recv.at[g], at_past(2 * ((y + d) % n_y) + core))
 
     run(1, to_chips)
-
-    def share(buffer, own, number, n, where):
-        for d in range(1, n):
-            block = buffer.at[own]
-            send(block, block, n_sem.at[number, 0], n_sem.at[number, 1], where((own + d) % n))
 
     def shared(buffer, number, n):
         wait_bytes(buffer.at[pl.ds(0, n - 1)], n_sem.at[number, 1])
@@ -282,36 +295,36 @@
             total = total + buffer[i]
         return total
 
-    share(norm_p, q, 0, n_past, at_past)
+    block = norm_p.at[x * n_past + q]
+    for d in plane:
+        send(block, block, n_sem.at[0, 0], n_sem.at[0, 1], at_plane(d))
     for g in range(groups):
         wait_bytes(rc.at[0, g, pl.ds(0, n_y - 1)], oy_recv.at[g])
         block = out_ref.at[pl.ds(g * size, size), :, core]
         send(block, block, oc_send.at[g], oc_recv.at[g], partner)
-    norm_x[x] = shared(norm_p, 0, n_past)
-    share(norm_x, x, 1, n_x, at_x)
-    norm_z[z] = shared(norm_x, 1, n_x)
-    share(norm_z, z, 2, n_z, at_z)
-    total = shared(norm_z, 2, n_z)
+    norm_z[z] = shared(norm_p, 0, n_x * n_past)
+    block = norm_z.at[z]
+    for d in far_first(n_z):
+        send(block, block, n_sem.at[1, 0], n_sem.at[1, 1], at_z((z + d) % n_z))
+    total = shared(norm_z, 1, n_z)
     mean = jnp.sum(total, axis=1, keepdims=True) * F32(1.0 / entries)
     norm_ref[0] = (jnp.sqrt(jnp.broadcast_to(mean, (1, LANES))) * F32(1.0 / STEP))[0, 0]
     for g in range(groups):
         wait_bytes(rc.at[0, g], oc_recv.at[g])
 
+    wait_bytes(rx, x_sem.at[0])
+    wait_bytes(rp.at[pl.ds(0, n_x * n_past - 1)], a_sem.at[0])
     for k in range(2):
-        wait_bytes(rx.at[k], x_sem.at[k, 0])
         wait_bytes(rz.at[k], z_sem.at[k, 0])
-        wait_bytes(win.at[k, 0, pl.ds(0, chunks - 1)], gz_sem.at[k, 0])
-        wait_bytes(win.at[k, pl.ds(0, n_x - 1)], gx_sem.at[k, 0])
+        wait_bytes(win.at[k, pl.ds(0, slots * chunks - 1)], g_sem.at[k, 0])
         for g in range(groups):
             wait_bytes(rc.at[k, g], c_send.at[k, g])
             wait_bytes(ry.at[k, g], y_send.at[k, g])
     for g in range(groups):
         wait_bytes(rc.at[0, g, pl.ds(0, n_y - 1)], oy_send.at[g])
         wait_bytes(rc.at[0, g], oc_send.at[g])
-    wait_bytes(zs.at[1, pl.ds(0, n_past - 1)], a_sem.at[0])
-    wait_bytes(norm_p.at[pl.ds(0, n_past - 1)], n_sem.at[0, 0])
-    wait_bytes(norm_x.at[pl.ds(0, n_x - 1)], n_sem.at[1, 0])
-    wait_bytes(norm_z.at[pl.ds(0, n_z - 1)], n_sem.at[2, 0])
+    wait_bytes(norm_p.at[pl.ds(0, n_x * n_past - 1)], n_sem.at[0, 0])
+    wait_bytes(norm_z.at[pl.ds(0, n_z - 1)], n_sem.at[1, 0])
 
 
 def local(n_past, n_second, green_row, green_hist, hamiltonian, quad_table, weight_index, block_start):
@@ -339,31 +352,29 @@
         pltpu.VMEM((2 * LANES, depth), BF16),
         pltpu.VMEM((LANES, LANES), BF16),
         pltpu.VMEM((2, n_x, n_past, rows, LANES), F32),
-        pltpu.VMEM((2, n_x - 1, n_past, rows, LANES), F32),
-        pltpu.VMEM((n_past, rows, LANES), F32),
+        pltpu.VMEM((n_x - 1, n_past, rows, LANES), F32),
+        pltpu.VMEM((n_x * n_past, rows, LANES), F32),
         pltpu.VMEM((2, chunks, rows, LANES), F32),
         pltpu.VMEM((2, n_z - 1, rows, LANES), F32),
-        pltpu.VMEM((2, slots, chunks, rows, LANES), F32),
+        pltpu.VMEM((2, slots * chunks, rows, LANES), F32),
         pltpu.VMEM((2, groups, 2, n_y, size, rows, LANES), F32),
         pltpu.VMEM((2, groups, n_y, size, rows, LANES), F32),
         pltpu.VMEM((2, groups, n_y, size, rows, LANES), F32),
         pltpu.VMEM((2, groups, n_y - 1, size, rows, LANES), F32),
         pltpu.VMEM((max(tiles, n_past), rows, LANES), F32),
         pltpu.VMEM((tiles, rows, LANES), F32),
-        pltpu.VMEM((n_past, 1, LANES), F32),
-        pltpu.VMEM((n_x, 1, LANES), F32),
+        pltpu.VMEM((n_x * n_past, 1, LANES), F32),
         pltpu.VMEM((n_z, 1, LANES), F32),
         dma((2,)),
-        dma((2, 2)),
         dma((2,)),
-        dma((2, 2)),
+        dma((2,)),
         dma((2, 2)),
         dma((2, 2)),
         dma((2, groups)), dma((2, groups)),
         dma((2, groups)), dma((2, groups)),
         dma((groups,)), dma((groups,)),
         dma((groups,)), dma((groups,)),
-        dma((3, 2)),
+        dma((2, 2)),
     ]
     smem = pl.BlockSpec(memory_space=pltpu.SMEM)
     vmem = pl.BlockSpec(memory_space=pltpu.VMEM)
@@ -378,7 +389,7 @@
         out_specs=(vmem, smem),
         scratch_shapes=scratch,
         compiler_params=pltpu.CompilerParams(
-            collective_id=0, has_side_effects=True, vmem_limit_bytes=40 * 1024 * 1024
+            collective_id=0, has_side_effects=True, vmem_limit_bytes=60 * 1024 * 1024
         ),
     )(
         block_start, weight_index, quad_table,

time: 109 us -> 85 us (0.78)
  Pallas kernels: 99.8 us -> 79.9 us
  local copies, waits for them, and re-layouts: 5.49 us -> 1.89 us
    pallas_call x1, Pallas kernels: 99.8 us -> 79.9 us  [local(): pl.pallas_call(functools.partial(kernel, dims), out_shape=(jax.ShapeDtype...]
    unnamed x11 -> x1, local copies, waits for them, and re-layouts: 5.49 us -> 1.89 us
where the time goes in v2:
time: 85 us; the launch traced here: 84.7 us
  Pallas kernels  79.9 us (94%)
  between operations  2.98 us (4%)
  local copies, waits for them, and re-layouts  1.89 us (2%)
    pallas_call x1, Pallas kernels, local(): pl.pallas_call(functools.partial(kernel, dims), out_shape=(jax.ShapeDtype...  79.9 us
    unnamed x1, local copies, waits for them, and re-layouts  1.89 us

profile of v2, /device:TPU:1, one launch (start us, length us, event | category | flops | bytes accessed | tf_op | source)
XLA Modules:
  0.0 84.7 jit_solution(16420702885526477546)
XLA Ops:
  1.3 79.9 %shard_map.77 = (f32[16,4,2,8,128]{4,3,2,1,0:T(8,128)}, f32[1]{0:T(128)}) custom-call(s32[1]{0:T(128)S(6)} %copy.10.start_ref, s32[4]{0:T(128)} %index_ref.1, f32[8]{0:T(128)} %table_ref.1, f32[16,8,8,128]{3,2,1,0:T(8,128)} %bitcast.3, f32[4,16,64,128]{3,2,1,0:T(8,128)} %hist_hbm.1, f32[64,128]{1,0:T(8,128)} %ham_ref.1), custom_call_target="tpu_custom_call" | custom-call | tf_op jit(solution)/shard_map/pallas_call | solution.py:382
  81.1 1.9 %copy.11 = f32[16,64,128]{2,1,0:T(8,128)} copy(f32[16,64,128]{2,1,0:T(8,128)} %bitcast.2) | data formatting | bytes 1048576

commit v3 on v2

--- a/solution.py
+++ b/solution.py
@@ -10,6 +10,8 @@
 
 COUPLING = 0.5
 STEP = 0.25
+PRODUCTS = 1
+GROUPS = 4
 CHIPS_X = 4
 LANES = 128
 MESH = pl.DeviceIdType.MESH
@@ -37,11 +39,11 @@
 
 
 def kernel(
-    dims, start_ref, index_ref, table_ref, row_hbm, hist_hbm, ham_ref, out_ref, norm_ref,
-    row, hist, r_high, r_low, r_ham, left, l_ham, cx, rx, rp, zs, rz, win,
-    part, rc, sc, ry, slope, pred, norm_p, norm_z,
-    in_sem, x_sem, a_sem, z_sem, g_sem, c_send, c_recv, y_send, y_recv,
-    oy_send, oy_recv, oc_send, oc_recv, n_sem,
+    dims, start_ref, index_hbm, table_hbm, row_hbm, hist_hbm, ham_hbm, out_hbm, norm_ref,
+    index_ref, table_ref, row, hist, ham_ref, near, early, r_high, r_low, r_ham, left, l_ham, cx, rx, rp, zs, rz, win,
+    part, rc, sc, ry, slope, pred, norm_p, norm_z, out,
+    in_sem, x_sem, near_sem, a_sem, z_sem, g_sem, c_send, c_recv, y_send, y_recv,
+    oy_send, oy_recv, oc_send, oc_recv, n_sem, out_sem,
 ):
     n_past, n_x, n_z, chunks, slots, tiles, groups, norm_scale, entries = dims
     n_y = n_past // 2
@@ -69,10 +71,12 @@
     plane.sort(key=lambda d: -min(d[0], n_y - d[0]) - min(d[2], n_x - d[2]))
     partner = at_past(2 * y + (1 - core))
 
-    row_copy = pltpu.make_async_copy(row_hbm, row, in_sem.at[0])
-    row_copy.start()
-    hist_copy = pltpu.make_async_copy(hist_hbm, hist, in_sem.at[1])
-    hist_copy.start()
+    copies = []
+    for source, target in (
+        (row_hbm, row), (hist_hbm, hist), (ham_hbm, ham_ref),
+        (index_hbm, index_ref), (table_hbm, table_ref),
+    ):
+        copies.append(pltpu.make_async_copy(source, target, in_sem.at[len(copies)]))
 
     barrier = pltpu.get_barrier_semaphore()
     reach = min(chunks // 2, n_z // 2)
@@ -87,6 +91,9 @@
     for other in others:
         pl.semaphore_signal(barrier, inc=1, device_id=other, device_id_type=MESH)
 
+    for copy in copies:
+        copy.start()
+
     lane = lax.broadcasted_iota(jnp.int32, (1, LANES), 1)
     real = lane < half
     turn = jnp.where(real, F32(1), F32(-1))
@@ -124,6 +131,21 @@
         for i in range(1, n_x):
             total = total + rp[pl.ds(i * n_past, n_past)]
         return total
+
+    def spread_near():
+        for e in (1, n_z - 1, 0):
+            for d in far_first(n_x) + [0]:
+                if d or e:
+                    slot = (0 if e == 0 else 1 if e == 1 else 2) * n_x + x
+                    where = (q, (z + e) % n_z * n_x + (x + d) % n_x)
+                    send(zs.at[0], near.at[slot], near_sem.at[0], near_sem.at[1], where)
+        near[x] = zs[0]
+
+    def near_done():
+        wait_bytes(near.at[pl.ds(0, 3 * n_x - 1)], near_sem.at[1])
+
+    def near_tile(t):
+        return (near[t] + near[n_x + t] + near[2 * n_x + t]).reshape(half, LANES)
 
     def scatter_z(k):
         for d in far_first(n_z):
@@ -146,6 +168,9 @@
     def window_done(k):
         wait_bytes(win.at[k, pl.ds(0, slots * chunks - 1)], g_sem.at[k, 1])
 
+    def window_tile(k):
+        return lambda t: win[k, pl.ds(t * chunks, chunks)].reshape(half, LANES)
+
 
     def prepare_hist(first, last):
         def body(s, carry):
@@ -178,10 +203,10 @@
         both = jnp.concatenate([high, low, high, jnp.zeros_like(high)], axis=0)
         r_ham[pl.ds(0, 4 * rows), pl.ds(s * LANES, LANES)] = both.astype(BF16)
 
-    def prepare_left(k):
+    def prepare_left(tile_of):
         for t in range(slots):
             weight = table_ref[index_ref[t]] * F32(norm_scale)
-            tile = win[k, pl.ds(t * chunks, chunks)].reshape(half, LANES)
+            tile = tile_of(t)
             first = weight * self_energy(tile)
             second = weight * tile
             real_part = jnp.where(real, first, swap(second))
@@ -190,18 +215,21 @@
             left[pl.ds(0, LANES), pl.ds(t * LANES, LANES)] = high.astype(BF16)
             left[pl.ds(LANES, LANES), pl.ds(t * LANES, LANES)] = low.astype(BF16)
 
-    def contract(k, g):
-        columns = pl.ds(g * size * LANES, size * LANES)
+    def contract(k, number):
+        wide = tiles // PRODUCTS
+        columns = pl.ds(number * wide * LANES, wide * LANES)
         both = jnp.dot(left[...], r_high[:, columns], preferred_element_type=F32)
         more = jnp.dot(left[pl.ds(0, LANES), :], r_low[:, columns], preferred_element_type=F32)
         ham = jnp.dot(l_ham[...], r_ham[:, columns], preferred_element_type=F32)
         total = both[:LANES] + both[LANES:] + more + ham
-        for s in range(size):
-            at = slice(s * LANES, (s + 1) * LANES)
+        for i in range(wide):
+            at = slice(i * LANES, (i + 1) * LANES)
             tile = total[:half, at] - turn * swap(total[half:, at])
+            g, s = divmod(number * wide + i, size)
             for p in range(n_past):
                 part[k, g, p % 2, p // 2, s] = tile[p * rows : (p + 1) * rows]
-        send(part.at[k, g, 1 - core], rc.at[k, g], c_send.at[k, g], c_recv.at[k, g], partner)
+            if s == size - 1:
+                send(part.at[k, g, 1 - core], rc.at[k, g], c_send.at[k, g], c_recv.at[k, g], partner)
 
     def between_chips(k, g):
         wait_bytes(rc.at[k, g], c_recv.at[k, g])
@@ -217,18 +245,19 @@
             total = total + ry[k, g, d]
         return turn * swap(total.reshape(size * rows, LANES)).reshape(size, rows, LANES)
 
-    def run(k, finish):
-        for g in range(groups + 1):
-            if g < groups:
-                contract(k, g)
-            if g >= 1:
-                between_chips(k, g - 1)
+    def integrate(k):
+        for number in range(PRODUCTS):
+            contract(k, number)
         for g in range(groups):
-            finish(g, slope_of(k, g))
+            between_chips(k, g)
+
+    def finish(k, use):
+        for g in range(groups):
+            use(g, slope_of(k, g))
 
 
     start = start_ref[0]
-    row_copy.wait()
+    copies[0].wait()
     for t in range(slots):
         wanted = start + slots * q + t - tiles * sec
         inside = (wanted >= 0) & (wanted < tiles)
@@ -236,57 +265,71 @@
         cx[0, t] = jnp.where(inside, tile, jnp.zeros_like(tile))
     pl.semaphore_wait(barrier, len(others))
     scatter_x()
+    copies[2].wait()
     prepare_ham()
     prepare_left_ham()
     for s in range(tiles):
         prepare_right_ham(s, row[s, q])
+    copies[1].wait()
+    prepare_hist(0, tiles)
     zs[0] = sum_x().reshape(zs.shape[1:])
+    spread_near()
     scatter_z(0)
-    hist_copy.wait()
-    prepare_hist(0, tiles // 2)
-    gather(0)
-    prepare_hist(tiles // 2, tiles)
-    window_done(0)
-    prepare_left(0)
-
-    def finish_first(g, values):
+    copies[3].wait()
+    copies[4].wait()
+    near_done()
+    prepare_left(near_tile)
+
+
+    def use_near(g, values):
+        for i in range(size):
+            s = g * size + i
+            early[s] = row[s, q] + F32(STEP) * values[i]
+
+    def use_first(g, values):
         for i in range(size):
             s = g * size + i
             slope[s] = values[i]
-            ahead = row[s, q] + F32(STEP) * values[i]
-            pred[s] = ahead
-
-    run(0, finish_first)
+            pred[s] = row[s, q] + F32(STEP) * values[i]
+
+    integrate(0)
+    gather(0)
+    finish(0, use_near)
 
 
     for p in range(slots * n_past):
         wanted = start + p - tiles * sec
         inside = (wanted >= 0) & (wanted < tiles)
-        tile = pred[jnp.clip(wanted, 0, tiles - 1)]
+        tile = early[jnp.clip(wanted, 0, tiles - 1)]
         cx[1, p % slots, p // slots] = jnp.where(inside, tile, jnp.zeros_like(tile))
     scatter_plane()
+    zs[1] = sum_plane()
+    scatter_z(1)
+    window_done(0)
+    prepare_left(window_tile(0))
+    integrate(1)
+    gather(1)
+    finish(1, use_first)
     for s in range(tiles):
         prepare_right_ham(s, pred[s])
-    zs[1] = sum_plane()
-    scatter_z(1)
-    gather(1)
     window_done(1)
-    prepare_left(1)
+    prepare_left(window_tile(1))
+    integrate(2)
 
     def to_chips(g, values):
         squares = jnp.zeros((rows, LANES), F32)
         for i in range(size):
             s = g * size + i
             after = row[s, q] + F32(0.5 * STEP) * (slope[s] + values[i])
-            out_ref[s, y, core] = after
+            out[s, y, core] = after
             change = after - pred[s]
             squares = squares + change * change
         norm_p[x * n_past + q] = (norm_p[x * n_past + q] if g else 0) + jnp.sum(squares, axis=0, keepdims=True)
-        block = out_ref.at[pl.ds(g * size, size), y, core]
+        block = out.at[pl.ds(g * size, size), y, core]
         for d in far_first(n_y):
             send(block, block, oy_send.at[g], oy_recv.at[g], at_past(2 * ((y + d) % n_y) + core))
 
-    run(1, to_chips)
+    finish(2, to_chips)
 
     def shared(buffer, number, n):
         wait_bytes(buffer.at[pl.ds(0, n - 1)], n_sem.at[number, 1])
@@ -300,23 +343,31 @@
         send(block, block, n_sem.at[0, 0], n_sem.at[0, 1], at_plane(d))
     for g in range(groups):
         wait_bytes(rc.at[0, g, pl.ds(0, n_y - 1)], oy_recv.at[g])
-        block = out_ref.at[pl.ds(g * size, size), :, core]
+        block = out.at[pl.ds(g * size, size), :, core]
         send(block, block, oc_send.at[g], oc_recv.at[g], partner)
     norm_z[z] = shared(norm_p, 0, n_x * n_past)
     block = norm_z.at[z]
     for d in far_first(n_z):
         send(block, block, n_sem.at[1, 0], n_sem.at[1, 1], at_z((z + d) % n_z))
+    results = []
+    for g in range(groups):
+        wait_bytes(rc.at[0, g], oc_recv.at[g])
+        block = pl.ds(g * size, size)
+        results.append(pltpu.make_async_copy(out.at[block], out_hbm.at[block], out_sem.at[g]))
+        results[-1].start()
     total = shared(norm_z, 1, n_z)
     mean = jnp.sum(total, axis=1, keepdims=True) * F32(1.0 / entries)
     norm_ref[0] = (jnp.sqrt(jnp.broadcast_to(mean, (1, LANES))) * F32(1.0 / STEP))[0, 0]
-    for g in range(groups):
-        wait_bytes(rc.at[0, g], oc_recv.at[g])
+    for result in results:
+        result.wait()
 
     wait_bytes(rx, x_sem.at[0])
+    wait_bytes(near.at[pl.ds(0, 3 * n_x - 1)], near_sem.at[0])
     wait_bytes(rp.at[pl.ds(0, n_x * n_past - 1)], a_sem.at[0])
     for k in range(2):
         wait_bytes(rz.at[k], z_sem.at[k, 0])
         wait_bytes(win.at[k, pl.ds(0, slots * chunks - 1)], g_sem.at[k, 0])
+    for k in range(3):
         for g in range(groups):
             wait_bytes(rc.at[k, g], c_send.at[k, g])
             wait_bytes(ry.at[k, g], y_send.at[k, g])
@@ -335,7 +386,7 @@
     n_y = n_past // 2
     rows = orbits // n_past
     chunks = n_past
-    groups = 4 if tiles % 4 == 0 and tiles > 4 else 2
+    groups = GROUPS if tiles > 4 else 2
     size = tiles // groups
     depth = 2 * slots * orbits
     dims = (
@@ -344,8 +395,13 @@
     )
     dma = pltpu.SemaphoreType.DMA
     scratch = [
+        pltpu.SMEM((slots,), jnp.int32),
+        pltpu.SMEM(quad_table.shape, F32),
         pltpu.VMEM((tiles, n_past, rows, LANES), F32),
         pltpu.VMEM((slots, tiles, orbits, LANES), F32),
+        pltpu.VMEM((orbits, LANES), F32),
+        pltpu.VMEM((3 * n_x, chunks, rows, LANES), F32),
+        pltpu.VMEM((tiles, rows, LANES), F32),
         pltpu.VMEM((depth, tiles * LANES), BF16),
         pltpu.VMEM((depth, tiles * LANES), BF16),
         pltpu.VMEM((LANES, tiles * LANES), BF16),
@@ -357,27 +413,29 @@
         pltpu.VMEM((2, chunks, rows, LANES), F32),
         pltpu.VMEM((2, n_z - 1, rows, LANES), F32),
         pltpu.VMEM((2, slots * chunks, rows, LANES), F32),
-        pltpu.VMEM((2, groups, 2, n_y, size, rows, LANES), F32),
-        pltpu.VMEM((2, groups, n_y, size, rows, LANES), F32),
-        pltpu.VMEM((2, groups, n_y, size, rows, LANES), F32),
-        pltpu.VMEM((2, groups, n_y - 1, size, rows, LANES), F32),
+        pltpu.VMEM((3, groups, 2, n_y, size, rows, LANES), F32),
+        pltpu.VMEM((3, groups, n_y, size, rows, LANES), F32),
+        pltpu.VMEM((3, groups, n_y, size, rows, LANES), F32),
+        pltpu.VMEM((3, groups, n_y - 1, size, rows, LANES), F32),
         pltpu.VMEM((max(tiles, n_past), rows, LANES), F32),
         pltpu.VMEM((tiles, rows, LANES), F32),
         pltpu.VMEM((n_x * n_past, 1, LANES), F32),
         pltpu.VMEM((n_z, 1, LANES), F32),
+        pltpu.VMEM((tiles, n_y, 2, rows, LANES), F32),
+        dma((5,)),
         dma((2,)),
         dma((2,)),
         dma((2,)),
         dma((2, 2)),
         dma((2, 2)),
-        dma((2, groups)), dma((2, groups)),
-        dma((2, groups)), dma((2, groups)),
+        dma((3, groups)), dma((3, groups)),
+        dma((3, groups)), dma((3, groups)),
         dma((groups,)), dma((groups,)),
         dma((groups,)), dma((groups,)),
         dma((2, 2)),
+        dma((groups,)),
     ]
     smem = pl.BlockSpec(memory_space=pltpu.SMEM)
-    vmem = pl.BlockSpec(memory_space=pltpu.VMEM)
     anywhere = pl.BlockSpec(memory_space=pl.ANY)
     after, change = pl.pallas_call(
         functools.partial(kernel, dims),
@@ -385,8 +443,8 @@
             jax.ShapeDtypeStruct((tiles, n_y, 2, rows, LANES), F32),
             jax.ShapeDtypeStruct((1,), F32),
         ),
-        in_specs=[smem, smem, smem, anywhere, anywhere, vmem],
-        out_specs=(vmem, smem),
+        in_specs=[smem] + [anywhere] * 5,
+        out_specs=(anywhere, smem),
         scratch_shapes=scratch,
         compiler_params=pltpu.CompilerParams(
             collective_id=0, has_side_effects=True, vmem_limit_bytes=60 * 1024 * 1024

time: 85 us -> 77.2 us (0.908)
  Pallas kernels: 79.9 us -> 72.1 us
    pallas_call x1, Pallas kernels: 79.9 us -> 72.1 us  [local(): pl.pallas_call(functools.partial(kernel, dims), out_shape=(jax.ShapeDtype...]
where the time goes in v3:
time: 77.2 us; the launch traced here: 77 us
  Pallas kernels  72.1 us (93%)
  between operations  2.98 us (4%)
  local copies, waits for them, and re-layouts  1.89 us (2%)
    pallas_call x1, Pallas kernels, local(): pl.pallas_call(functools.partial(kernel, dims), out_shape=(jax.ShapeDtype...  72.1 us
    unnamed x1, local copies, waits for them, and re-layouts  1.89 us

profile of v3, /device:TPU:1, one launch (start us, length us, event | category | flops | bytes accessed | tf_op | source)
XLA Modules:
  0.0 77.0 jit_solution(8496860092386489495)
XLA Ops:
  1.3 72.1 %shard_map.77 = (f32[16,4,2,8,128]{4,3,2,1,0:T(8,128)}, f32[1]{0:T(128)}) custom-call(s32[1]{0:T(128)S(6)} %copy.10.start_ref, s32[4]{0:T(128)} %index_hbm.1, f32[8]{0:T(128)} %table_hbm.1, f32[16,8,8,128]{3,2,1,0:T(8,128)} %bitcast.3, f32[4,16,64,128]{3,2,1,0:T(8,128)} %hist_hbm.1, f32[64,128]{1,0:T(8,128)} %ham_hbm.1), custom_call_target="tpu_custom_call" | custom-call | tf_op jit(solution)/shard_map/pallas_call | solution.py:440
  73.4 1.9 %copy.11 = f32[16,64,128]{2,1,0:T(8,128)} copy(f32[16,64,128]{2,1,0:T(8,128)} %bitcast.2) | data formatting | bytes 1048576

commit v4 on v3

--- a/solution.py
+++ b/solution.py
@@ -78,6 +78,7 @@
     ):
         copies.append(pltpu.make_async_copy(source, target, in_sem.at[len(copies)]))
 
+    copies[0].start()
     barrier = pltpu.get_barrier_semaphore()
     reach = min(chunks // 2, n_z // 2)
     others = [at_z((z + d) % n_z) for d in far_first(n_z)]
@@ -91,8 +92,6 @@
     for other in others:
         pl.semaphore_signal(barrier, inc=1, device_id=other, device_id_type=MESH)
 
-    for copy in copies:
-        copy.start()
 
     lane = lax.broadcasted_iota(jnp.int32, (1, LANES), 1)
     real = lane < half
@@ -231,12 +230,14 @@
             if s == size - 1:
                 send(part.at[k, g, 1 - core], rc.at[k, g], c_send.at[k, g], c_recv.at[k, g], partner)
 
-    def between_chips(k, g):
-        wait_bytes(rc.at[k, g], c_recv.at[k, g])
-        sc[k, g] = part[k, g, core] + rc[k, g]
+    def between_chips(k):
+        for g in range(groups):
+            wait_bytes(rc.at[k, g], c_recv.at[k, g])
+            sc[k, g] = part[k, g, core] + rc[k, g]
         for d in far_first(n_y):
             to = (y + d) % n_y
-            send(sc.at[k, g, to], ry.at[k, g, d - 1], y_send.at[k, g], y_recv.at[k, g], at_past(2 * to + core))
+            for g in range(groups):
+                send(sc.at[k, g, to], ry.at[k, g, d - 1], y_send.at[k, g], y_recv.at[k, g], at_past(2 * to + core))
 
     def slope_of(k, g):
         wait_bytes(ry.at[k, g], y_recv.at[k, g])
@@ -248,8 +249,7 @@
     def integrate(k):
         for number in range(PRODUCTS):
             contract(k, number)
-        for g in range(groups):
-            between_chips(k, g)
+        between_chips(k)
 
     def finish(k, use):
         for g in range(groups):
@@ -258,6 +258,8 @@
 
     start = start_ref[0]
     copies[0].wait()
+    for copy in copies[1:]:
+        copy.start()
     for t in range(slots):
         wanted = start + slots * q + t - tiles * sec
         inside = (wanted >= 0) & (wanted < tiles)
@@ -325,9 +327,6 @@
             change = after - pred[s]
             squares = squares + change * change
         norm_p[x * n_past + q] = (norm_p[x * n_past + q] if g else 0) + jnp.sum(squares, axis=0, keepdims=True)
-        block = out.at[pl.ds(g * size, size), y, core]
-        for d in far_first(n_y):
-            send(block, block, oy_send.at[g], oy_recv.at[g], at_past(2 * ((y + d) % n_y) + core))
 
     finish(2, to_chips)
 
@@ -341,14 +340,18 @@
     block = norm_p.at[x * n_past + q]
     for d in plane:
         send(block, block, n_sem.at[0, 0], n_sem.at[0, 1], at_plane(d))
+    for d in far_first(n_y):
+        for g in range(groups):
+            block = out.at[pl.ds(g * size, size), y, core]
+            send(block, block, oy_send.at[g], oy_recv.at[g], at_past(2 * ((y + d) % n_y) + core))
+    norm_z[z] = shared(norm_p, 0, n_x * n_past)
+    block = norm_z.at[z]
+    for d in far_first(n_z):
+        send(block, block, n_sem.at[1, 0], n_sem.at[1, 1], at_z((z + d) % n_z))
     for g in range(groups):
         wait_bytes(rc.at[0, g, pl.ds(0, n_y - 1)], oy_recv.at[g])
         block = out.at[pl.ds(g * size, size), :, core]
         send(block, block, oc_send.at[g], oc_recv.at[g], partner)
-    norm_z[z] = shared(norm_p, 0, n_x * n_past)
-    block = norm_z.at[z]
-    for d in far_first(n_z):
-        send(block, block, n_sem.at[1, 0], n_sem.at[1, 1], at_z((z + d) % n_z))
     results = []
     for g in range(groups):
         wait_bytes(rc.at[0, g], oc_recv.at[g])

time: 77.2 us -> 77.1 us (level)
  no operation moved by 1% of the time
where the time goes in v4:
time: 77.1 us; the launch traced here: 76.9 us
  Pallas kernels  72 us (93%)
  between operations  2.98 us (4%)
  local copies, waits for them, and re-layouts  1.89 us (2%)
    pallas_call x1, Pallas kernels, local(): pl.pallas_call(functools.partial(kernel, dims), out_shape=(jax.ShapeDtype...  72 us
    unnamed x1, local copies, waits for them, and re-layouts  1.89 us

profile of v4, /device:TPU:1, one launch (start us, length us, event | category | flops | bytes accessed | tf_op | source)
XLA Modules:
  0.0 76.9 jit_solution(7221492745989286352)
XLA Ops:
  1.3 72.0 %shard_map.77 = (f32[16,4,2,8,128]{4,3,2,1,0:T(8,128)}, f32[1]{0:T(128)}) custom-call(s32[1]{0:T(128)S(6)} %copy.10.start_ref, s32[4]{0:T(128)} %index_hbm.1, f32[8]{0:T(128)} %table_hbm.1, f32[16,8,8,128]{3,2,1,0:T(8,128)} %bitcast.3, f32[4,16,64,128]{3,2,1,0:T(8,128)} %hist_hbm.1, f32[64,128]{1,0:T(8,128)} %ham_hbm.1), custom_call_target="tpu_custom_call" | custom-call | tf_op jit(solution)/shard_map/pallas_call | solution.py:443
  73.3 1.9 %copy.11 = f32[16,64,128]{2,1,0:T(8,128)} copy(f32[16,64,128]{2,1,0:T(8,128)} %bitcast.2) | data formatting | bytes 1048576

commit v5 on v4

--- a/solution.py
+++ b/solution.py
@@ -131,20 +131,20 @@
             total = total + rp[pl.ds(i * n_past, n_past)]
         return total
 
+
     def spread_near():
-        for e in (1, n_z - 1, 0):
-            for d in far_first(n_x) + [0]:
-                if d or e:
-                    slot = (0 if e == 0 else 1 if e == 1 else 2) * n_x + x
-                    where = (q, (z + e) % n_z * n_x + (x + d) % n_x)
-                    send(zs.at[0], near.at[slot], near_sem.at[0], near_sem.at[1], where)
+        for to in range(n_x):
+            beside = (z + 1) % n_z if to < n_x // 2 else (z + n_z - 1) % n_z
+            send(zs.at[0], near.at[n_x + x], near_sem.at[0], near_sem.at[1], (q, beside * n_x + to))
+        for d in far_first(n_x):
+            send(zs.at[0], near.at[x], near_sem.at[0], near_sem.at[1], at_x((x + d) % n_x))
         near[x] = zs[0]
 
     def near_done():
-        wait_bytes(near.at[pl.ds(0, 3 * n_x - 1)], near_sem.at[1])
+        wait_bytes(near.at[pl.ds(0, 2 * n_x - 1)], near_sem.at[1])
 
     def near_tile(t):
-        return (near[t] + near[n_x + t] + near[2 * n_x + t]).reshape(half, LANES)
+        return (near[t] + near[n_x + t]).reshape(half, LANES)
 
     def scatter_z(k):
         for d in far_first(n_z):
@@ -365,7 +365,7 @@
         result.wait()
 
     wait_bytes(rx, x_sem.at[0])
-    wait_bytes(near.at[pl.ds(0, 3 * n_x - 1)], near_sem.at[0])
+    wait_bytes(near.at[pl.ds(0, 2 * n_x - 1)], near_sem.at[0])
     wait_bytes(rp.at[pl.ds(0, n_x * n_past - 1)], a_sem.at[0])
     for k in range(2):
         wait_bytes(rz.at[k], z_sem.at[k, 0])
@@ -403,7 +403,7 @@
         pltpu.VMEM((tiles, n_past, rows, LANES), F32),
         pltpu.VMEM((slots, tiles, orbits, LANES), F32),
         pltpu.VMEM((orbits, LANES), F32),
-        pltpu.VMEM((3 * n_x, chunks, rows, LANES), F32),
+        pltpu.VMEM((2 * n_x, chunks, rows, LANES), F32),
         pltpu.VMEM((tiles, rows, LANES), F32),
         pltpu.VMEM((depth, tiles * LANES), BF16),
         pltpu.VMEM((depth, tiles * LANES), BF16),

time: 77.1 us -> 76.5 us (level)
  no operation moved by 1% of the time
where the time goes in v5:
time: 76.5 us; the launch traced here: 76.3 us
  Pallas kernels  71.4 us (93%)
  between operations  2.98 us (4%)
  local copies, waits for them, and re-layouts  1.89 us (2%)
    pallas_call x1, Pallas kernels, local(): pl.pallas_call(functools.partial(kernel, dims), out_shape=(jax.ShapeDtype...  71.4 us
    unnamed x1, local copies, waits for them, and re-layouts  1.89 us

profile of v5, /device:TPU:1, one launch (start us, length us, event | category | flops | bytes accessed | tf_op | source)
XLA Modules:
  0.0 76.3 jit_solution(3280338945716110663)
XLA Ops:
  1.3 71.4 %shard_map.77 = (f32[16,4,2,8,128]{4,3,2,1,0:T(8,128)}, f32[1]{0:T(128)}) custom-call(s32[1]{0:T(128)S(6)} %copy.10.start_ref, s32[4]{0:T(128)} %index_hbm.1, f32[8]{0:T(128)} %table_hbm.1, f32[16,8,8,128]{3,2,1,0:T(8,128)} %bitcast.3, f32[4,16,64,128]{3,2,1,0:T(8,128)} %hist_hbm.1, f32[64,128]{1,0:T(8,128)} %ham_hbm.1), custom_call_target="tpu_custom_call" | custom-call | tf_op jit(solution)/shard_map/pallas_call | solution.py:443
  72.7 1.9 %copy.11 = f32[16,64,128]{2,1,0:T(8,128)} copy(f32[16,64,128]{2,1,0:T(8,128)} %bitcast.2) | data formatting | bytes 1048576
